TPU v7x, 32 devices: a whole 2x2x4 slice. The times are simulated.
32 devices in a mesh: blk: 8 (over z, y), grp: 4 (over x, core).
Axes of the slice: x: 2, y: 2, z: 4, core: 2. Of those that a mesh axis runs over, the one named last changes fastest.
Arguments:
- view_spectra: bfloat16 [8, 2, 128, 128], P('blk', None, 'grp'), may hold values from -6 to 6
- search_states: int32 [8], P('blk'), may hold values from 0 to 3
- micrograph_spectra: bfloat16 [16, 2, 128, 128], P('blk'), may hold values from -6 to 6
- defocus: float32 [8], replicated, may hold values from 20 to 60
- micrograph_group: int32 [2], replicated, may hold values from 0 to 7
Outputs:
- peak_map: float32 [16, 256, 256], P('blk', 'grp')
- zscore_map: float32 [16, 256, 256], P('blk', 'grp')
All inputs are finite; a program needn't handle non-finite values.
Results may differ from a plain program's by a relative error of at most 0.0035.
Values may be sent and summed in bfloat16 or wider, within the bound.
A program may use at most 64 MiB of HBM per device.

v0:
```python
import jax
import jax.numpy as jnp
from jax import lax
from jax.sharding import PartitionSpec as P

BOX = 256
KF = 128
MICROGRAPHS = 2
GROUPS = 8


focus_offset = 3.0
phase_shift = 0.1


def dft_tables(positions):
    frequency = jnp.arange(KF, dtype=jnp.int32)[None, :] - KF // 2
    phase = jnp.mod(positions[:, None] * frequency, BOX).astype(jnp.float32) * (2.0 * jnp.pi / BOX)
    return (jnp.cos(phase).astype(jnp.bfloat16), jnp.sin(phase).astype(jnp.bfloat16))


def radius_grid():
    frequency = (jnp.arange(KF, dtype=jnp.int32) - KF // 2).astype(jnp.float32)
    return (frequency[:, None] ** 2 + frequency[None, :] ** 2) / float(KF * KF)


def per_device(view_spectra, search_states, micrograph_spectra, defocus, micrograph_group):
    columns = BOX // lax.axis_size("grp")
    col_start = lax.axis_index("grp") * columns
    cos_x, sin_x = dft_tables(col_start + jnp.arange(columns, dtype=jnp.int32))
    cos_y, sin_y = dft_tables(jnp.arange(BOX, dtype=jnp.int32))
    left_table = jnp.concatenate(
        [jnp.concatenate([cos_x, -sin_x], axis=1), jnp.concatenate([sin_x, cos_x], axis=1)], axis=0
    )
    radius_sq = radius_grid()
    tiles_here = micrograph_spectra.shape[0]
    blocks = lax.axis_size("blk")
    tile_total = tiles_here * blocks
    tile_ids = lax.axis_index("blk") * tiles_here + jnp.arange(tiles_here, dtype=jnp.int32)
    micro_ids = tile_ids // (tile_total // MICROGRAPHS)
    micro_onehot = micro_ids[:, None] == jnp.arange(MICROGRAPHS, dtype=jnp.int32)[None, :]
    group_ids = jnp.sum(jnp.where(micro_onehot, micrograph_group[None, :], 0), axis=1)
    group_onehot = group_ids[:, None] == jnp.arange(GROUPS, dtype=jnp.int32)[None, :]
    base_focus = jnp.sum(jnp.where(group_onehot, defocus[None, :], 0.0), axis=1)
    micro_real = micrograph_spectra[:, 0].astype(jnp.float32)
    micro_imag = micrograph_spectra[:, 1].astype(jnp.float32)
    flip_sign = (1 - 2 * jnp.mod(search_states, 2)).astype(jnp.bfloat16)
    signed_views = jnp.stack(
        [view_spectra[:, 0], view_spectra[:, 1] * flip_sign[:, None, None]], axis=1
    )
    focus_flags = (search_states // 2).astype(jnp.bfloat16)

    def score_view(running, scan_input):
        spectrum, focus_flag = scan_input
        real_part = spectrum[0].astype(jnp.float32)
        imag_part = spectrum[1].astype(jnp.float32)
        defocus_now = base_focus + focus_offset * (2.0 * focus_flag.astype(jnp.float32) - 1.0)
        transfer = -jnp.sin(defocus_now[:, None, None] * radius_sq[None] + phase_shift)
        prod_real = (transfer * (real_part * micro_real + imag_part * micro_imag)).astype(
            jnp.bfloat16
        )
        prod_imag = (transfer * (real_part * micro_imag - imag_part * micro_real)).astype(
            jnp.bfloat16
        )
        stacked = jnp.concatenate([prod_real, prod_imag], axis=1)
        section_one = jnp.einsum(
            "ab,tbk->tak", left_table, stacked, preferred_element_type=jnp.float32
        ).astype(jnp.bfloat16)
        part_a = section_one[:, :columns]
        part_b = section_one[:, columns:]
        scores = (
            jnp.einsum("txk,yk->txy", part_a, cos_y, preferred_element_type=jnp.float32)
            - jnp.einsum("txk,yk->txy", part_b, sin_y, preferred_element_type=jnp.float32)
        ) / KF
        peak_map, totals, squares = running
        return ((jnp.maximum(peak_map, scores), totals + scores, squares + scores * scores), None)

    shape = (tiles_here, columns, BOX)
    start_state = (
        jnp.full(shape, -1e30, jnp.float32),
        jnp.zeros(shape, jnp.float32),
        jnp.zeros(shape, jnp.float32),
    )
    full_views = lax.all_gather(signed_views, "grp", axis=2, tiled=True)
    result, unused = lax.scan(
        score_view,
        start_state,
        (
            lax.all_gather(full_views, "blk", axis=0, tiled=True),
            lax.all_gather(focus_flags, "blk", axis=0, tiled=True),
        ),
    )
    running = result
    peak_map, totals, squares = running
    view_total = blocks * view_spectra.shape[0]
    mean_map = totals / view_total
    variance = squares / view_total - mean_map * mean_map
    zscore_map = (peak_map - mean_map) / jnp.sqrt(variance + 1e-05)
    return (peak_map, zscore_map)


def solution(mesh):
    return jax.shard_map(
        per_device,
        mesh=mesh,
        in_specs=(P("blk", None, "grp", None), P("blk"), P("blk", None, None, None), P(), P()),
        out_specs=(P("blk", "grp", None), P("blk", "grp", None)),
        check_vma=False,
    )
```

profile of v0, /device:TPU:0, one launch (start us, length us, event | category | flops | bytes accessed | tf_op | source)
XLA Modules:
  0.0 97.1 jit_solution(1618560314489117984)
XLA Ops:
  1.3 0.6 copy-done.5
  2.5 0.7 copy-done.3
  7.4 1.3 %dynamic-update-slice = bf16[8]{0:T(256)(128)(2,1)S(1)} dynamic-update-slice(bf16[8]{0:T(256)(128)(2,1)S(1)} %broadcast.120, bf16[1]{0:T(256)(128)(2,1)} %get-tuple-element.316, u32[]{:T(128)} %bitcast) | dynamic-update-slice | bytes 8
  8.8 23.1 %all-reduce = bf16[8]{0:T(256)(128)(2,1)S(1)} all-reduce(bf16[8]{0:T(256)(128)(2,1)S(1)} %dynamic-update-slice), channel_id=1, replica_groups=mesh['blk'=8,'grp'=4] {'blk'}, use_global_device_ids=true, to_apply=%add | all-reduce | flops 8 | bytes 32
  32.4 5.2 %all_gather.10 = bf16[1,2,128,128]{3,2,1,0:T(8,128)(2,1)S(1)} all-gather(bf16[1,2,32,128]{3,2,1,0:T(8,128)(2,1)S(1)} %pad_maximum_fusion), channel_id=1, replica_groups=mesh['blk'=8,'grp'=4] {'grp'}, dimensions={2}, use_global_device_ids=true | all-gather | bytes 81920 | tf_op jit(solution)/shard_map/all_gather | solution.py:84
  37.6 31.3 %all_gather.11 = bf16[8,2,128,128]{3,2,1,0:T(8,128)(2,1)S(1)} all-gather(bf16[1,2,128,128]{3,2,1,0:T(8,128)(2,1)S(1)} %all_gather.10), channel_id=1, replica_groups=mesh['blk'=8,'grp'=4] {'blk'}, dimensions={0}, use_global_device_ids=true | all-gather | bytes 589824 | tf_op jit(solution)/shard_map/all_gather | solution.py:89
  69.0 27.5 %while.19 = (s32[]{:T(128)}, f32[2,64,256]{2,1,0:T(8,128)S(1)}, f32[2,64,256]{2,1,0:T(8,128)S(1)}, f32[2,64,256]{2,1,0:T(8,128)S(1)}, bf16[8]{0:T(256)(128)(2,1)...) while((s32[]{:T(128)}, f32[2,64,256]{2,1,0:T(8,128)S(1)}, ...), condition=%wide.region_3.4_spmd.clone.clone.clone, body=%wide.region_2.3_spmd.clone.clone.clone.sunk | while | flops 35618824 | bytes 2230033 | solution.py:85
  71.1 0.6 fusion.59
  71.7 0.7 select_add_fusion.3
  74.5 0.6 fusion.59
  75.1 0.7 select_add_fusion.3
  77.9 0.6 fusion.59
  78.6 0.7 select_add_fusion.3
  81.4 0.6 fusion.59
  82.0 0.7 select_add_fusion.3
  84.8 0.6 fusion.59
  85.4 0.7 select_add_fusion.3
  88.2 0.6 fusion.59
  88.9 0.7 select_add_fusion.3
  91.7 0.6 fusion.59
  92.3 0.7 select_add_fusion.3
  95.1 0.6 fusion.59
  95.7 0.7 select_add_fusion.3
  96.4 0.7 rsqrt_multiply_fusion
  (76 shorter events, 13.9 us)
Async XLA Ops:
  1.3 0.7 copy-start.5
  2.5 0.7 copy-start.3
  3.2 0.7 copy-start.4
  4.0 27.9 %copy-start.2 = (bf16[1,2,32,128]{3,2,1,0:T(8,128)(2,1)S(1)}, bf16[1,2,32,128]{3,2,1,0:T(8,128)(2,1)}, u32[]{:S(2)}) copy-start(bf16[1,2,32,128]{3,2,1,0:T(8,128)(2,1)} %param.7) | copy-start | bytes 49156
  31.9 5.7 %copy-start.1 = (bf16[2,2,128,128]{3,2,1,0:T(8,128)(2,1)S(1)}, bf16[2,2,128,128]{3,2,1,0:T(8,128)(2,1)}, u32[]{:S(2)}) copy-start(bf16[2,2,128,128]{3,2,1,0:T(8,128)(2,1)} %param.9) | copy-start | bytes 393220
  96.4 0.7 copy-start
where the time goes:
time: 97.5 us; the launch traced here: 97.1 us
  blocking collectives  59.7 us (61%)
  matrix products  11.7 us (12%)
  local copies, waits for them, and re-layouts  8.39 us (9%)
  other arithmetic  7.45 us (8%)
  loops' own time  5.72 us (6%)
  between operations  4.16 us (4%)
    all_gather x1, blocking collectives, per_device(): lax.all_gather(full_views, 'blk', axis=0, tiled=True)  31.3 us
    unnamed x1, blocking collectives  23.1 us
    another operation x1, loops' own time, per_device(): lax.scan(score_view, start_state, (lax.all_gather(full_views, 'blk', axis...  5.72 us
    dot_general x8, matrix products, score_view(): jnp.einsum('txk,yk->txy', part_b, sin_y, preferred_element_type=jnp.float32)  5.39 us
    all_gather x1, blocking collectives, per_device(): full_views = lax.all_gather(signed_views, 'grp', axis=2, tiled=True)  5.25 us
    dot_general x8, matrix products, score_view(): jnp.einsum('txk,yk->txy', part_a, cos_y, preferred_element_type=jnp.float32)  4.99 us
    dynamic_slice x8, local copies, waits for them, and re-layouts, per_device(): lax.scan(score_view, start_state, (lax.all_gather(full_views, 'blk', axis...  4.71 us
    convert_element_type x8, other arithmetic, score_view(): (transfer * (real_part * micro_real + imag_part * micro_imag)).astype(jnp...  4.48 us

commit v1 on v0

v1 whole, which is shorter than its diff:
```python
import functools
import math

import jax
import jax.numpy as jnp
import ml_dtypes
import numpy as np
from jax import lax
from jax.experimental import pallas as pl
from jax.experimental.pallas import tpu as pltpu
from jax.sharding import PartitionSpec as P

BOX = 256
KF = 128
MICROGRAPHS = 2
focus_offset = 3.0
phase_shift = 0.1
MESH = pl.DeviceIdType.MESH
f32, bf16 = jnp.float32, jnp.bfloat16


def dft_tables():
    position = np.arange(BOX)[:, None]
    frequency = np.arange(KF)[None, :] - KF // 2
    phase = np.mod(position * frequency, BOX) * (2.0 * np.pi / BOX)
    return np.cos(phase), np.sin(phase)


def constant_tables(groups):
    cos, sin = dft_tables()
    columns = BOX // groups
    left = []
    for g in range(groups):
        c, s = (tab[g * columns : (g + 1) * columns] for tab in (cos, sin))
        left.append(np.block([[c, -s], [s, c]]))
    right = np.concatenate([cos.T, -sin.T], axis=0) / KF
    return np.stack(left).astype(ml_dtypes.bfloat16), right.astype(ml_dtypes.bfloat16)


def flip_bits(index, mask, size):
    bits = int(math.log2(size))
    return sum(((index // 2**i + mask // 2**i) % 2) * 2**i for i in range(bits))


def kernel(
    n,
    groups,
    tiles,
    views_ref,
    states_ref,
    micro_ref,
    defocus_ref,
    group_ref,
    left_ref,
    right_ref,
    peak_ref,
    zscore_ref,
    spectra,
    flags,
    filtered,
    totals,
    squares,
    blk_send,
    blk_recv,
    flag_send,
    flag_recv,
    x_send,
    x_recv,
    core_send,
    core_recv,
    far_send,
    far_recv,
):
    b, g = lax.axis_index("blk"), lax.axis_index("grp")
    g_core = g + 1 - 2 * (g % 2)
    g_x = (g + 2) % groups
    g_far = (g_core + 2) % groups
    rows = views_ref.shape[2]
    columns = BOX // groups
    unroll = n <= 8

    def each(low, high, body):
        if unroll:
            for d in range(low, high):
                body(d)
        else:
            lax.fori_loop(low, high, lambda d, carry: (body(d), carry)[1], 0)

    def peer(d):
        return flip_bits(b, d, n)

    def to(block, group):
        return dict(device_id=(block, group), device_id_type=MESH)

    def blk_copy(d, source):
        part = spectra.at[source, g]
        return pltpu.make_async_remote_copy(
            part, part, blk_send.at[d], blk_recv.at[d], **to(peer(d), g)
        )

    def flag_copy(d, source):
        part = flags.at[source]
        return pltpu.make_async_remote_copy(
            part, part, flag_send.at[d], flag_recv.at[d], **to(peer(d), g)
        )

    def x_copy(d, group):
        part = spectra.at[peer(d), group]
        return pltpu.make_async_remote_copy(
            part, part, x_send.at[d], x_recv.at[d], **to(b, g_x)
        )

    def core_copy(d, group):
        part = spectra.at[peer(d), group]
        return pltpu.make_async_remote_copy(
            part, part, core_send.at[d], core_recv.at[d], **to(b, g_core)
        )

    def far_copy(d, group):
        part = spectra.at[peer(d), group]
        return pltpu.make_async_remote_copy(
            part, part, far_send.at[d], far_recv.at[d], **to(b, g_core)
        )

    barrier = pltpu.get_barrier_semaphore()
    each(1, n, lambda d: pl.semaphore_signal(barrier, inc=1, **to(peer(d), g)))
    pl.semaphore_signal(barrier, inc=1, **to(b, g_x))
    pl.semaphore_signal(barrier, inc=1, **to(b, g_core))

    state = states_ref[0]
    flip = (1 - 2 * (state % 2)).astype(f32)
    spectra[b, g, 0] = views_ref[0, 0]
    spectra[b, g, 1] = (views_ref[0, 1].astype(f32) * flip).astype(bf16)
    flags[b] = jnp.full((1, KF), (state // 2).astype(f32), f32)
    pl.semaphore_wait(barrier, n + 1)

    x_copy(0, g).start()
    core_copy(0, g).start()

    def send_own(d):
        blk_copy(d, b).start()
        flag_copy(d, b).start()

    each(1, n, send_own)

    micro = (b * tiles) // (n * tiles // MICROGRAPHS)
    base = defocus_ref[group_ref[micro]]
    row_f = (lax.broadcasted_iota(jnp.int32, (KF, KF), 0) - KF // 2).astype(f32)
    col_f = (lax.broadcasted_iota(jnp.int32, (KF, KF), 1) - KF // 2).astype(f32)
    radius_sq = (row_f * row_f + col_f * col_f) * (1.0 / (KF * KF))
    for step in range(2):
        transfer = -jnp.sin((base + focus_offset * (2.0 * step - 1.0)) * radius_sq + phase_shift)
        for t in range(tiles):
            for part in range(2):
                filtered[step, t, part] = transfer * micro_ref[t, part].astype(f32)

    def forward_blk(d):
        blk_copy(d, peer(d)).wait_recv()
        x_copy(d, g).start()
        core_copy(d, g).start()

    def forward_x(d):
        x_copy(d, g_x).wait_recv()
        far_copy(d, g_x).start()

    def score(d, first):
        v = peer(d)
        core_copy(d, g_core).wait_recv()
        far_copy(d, g_far).wait_recv()
        real = spectra[v, :, 0].reshape(KF, KF).astype(f32)
        imag = spectra[v, :, 1].reshape(KF, KF).astype(f32)
        later = jnp.broadcast_to(flags[v], (KF, KF)) > 0.5
        stacks = []
        for t in range(tiles):
            m_real = jnp.where(later, filtered[1, t, 0], filtered[0, t, 0])
            m_imag = jnp.where(later, filtered[1, t, 1], filtered[0, t, 1])
            prod_real = (real * m_real + imag * m_imag).astype(bf16)
            prod_imag = (real * m_imag - imag * m_real).astype(bf16)
            stacks.append(jnp.concatenate([prod_real, prod_imag], axis=0))
        stacked = jnp.concatenate(stacks, axis=1)
        section = jnp.dot(left_ref[g], stacked, preferred_element_type=f32).astype(bf16)
        lines = jnp.concatenate(
            [
                jnp.concatenate(
                    [
                        section[:columns, t * KF : (t + 1) * KF],
                        section[columns:, t * KF : (t + 1) * KF],
                    ],
                    axis=1,
                )
                for t in range(tiles)
            ],
            axis=0,
        )
        scores = jnp.dot(lines, right_ref[...], preferred_element_type=f32)
        scores = scores.reshape(tiles, columns, BOX)
        if first:
            peak_ref[...] = scores
            totals[...] = scores
            squares[...] = scores * scores
        else:
            peak_ref[...] = jnp.maximum(peak_ref[...], scores)
            totals[...] += scores
            squares[...] += scores * scores

    def wait_flag(d):
        flag_copy(d, peer(d)).wait_recv()

    if unroll:
        for d in range(n + 2):
            if 1 <= d < n:
                forward_blk(d)
            if 1 <= d <= n:
                forward_x(d - 1)
            if d >= 2:
                if d > 2:
                    wait_flag(d - 2)
                score(d - 2, d == 2)
    else:
        forward_x(0)

        def pump(d):
            forward_blk(d)
            wait_flag(d)

        each(1, n, pump)
        each(1, n, forward_x)
        score(0, True)
        each(1, n, lambda d: score(d, False))

    total = 1.0 / n
    mean = totals[...] * total
    variance = squares[...] * total - mean * mean
    zscore_ref[...] = (peak_ref[...] - mean) * lax.rsqrt(variance + 1e-5)

    def drain(d):
        x_copy(d, g).wait_send()
        core_copy(d, g).wait_send()
        far_copy(d, g_x).wait_send()

    def drain_own(d):
        blk_copy(d, b).wait_send()
        flag_copy(d, b).wait_send()

    each(0, n, drain)
    each(1, n, drain_own)


def solution(mesh):
    n, groups = mesh.shape["blk"], mesh.shape["grp"]
    left, right = constant_tables(groups)

    def per_device(view_spectra, search_states, micrograph_spectra, defocus, micrograph_group):
        tiles = micrograph_spectra.shape[0]
        rows = view_spectra.shape[2]
        columns = BOX // groups
        vmem = pl.BlockSpec(memory_space=pltpu.VMEM)
        smem = pl.BlockSpec(memory_space=pltpu.SMEM)
        out = jax.ShapeDtypeStruct((tiles, columns, BOX), f32)
        return pl.pallas_call(
            functools.partial(kernel, n, groups, tiles),
            out_shape=(out, out),
            in_specs=[vmem, smem, vmem, smem, smem, vmem, vmem],
            out_specs=(vmem, vmem),
            scratch_shapes=[
                pltpu.VMEM((n, groups, 2, rows, KF), bf16),
                pltpu.VMEM((n, 1, KF), f32),
                pltpu.VMEM((2, tiles, 2, KF, KF), f32),
                pltpu.VMEM((tiles, columns, BOX), f32),
                pltpu.VMEM((tiles, columns, BOX), f32),
            ]
            + [pltpu.SemaphoreType.DMA((n,))] * 10,
            compiler_params=pltpu.CompilerParams(
                collective_id=0, has_side_effects=True, vmem_limit_bytes=32 * 2**20
            ),
        )(
            view_spectra,
            search_states,
            micrograph_spectra,
            defocus,
            micrograph_group,
            jnp.asarray(left),
            jnp.asarray(right),
        )

    return jax.shard_map(
        per_device,
        mesh=mesh,
        in_specs=(P("blk", None, "grp", None), P("blk"), P("blk", None, None, None), P(), P()),
        out_specs=(P("blk", "grp", None), P("blk", "grp", None)),
        check_vma=False,
    )
```

time: 97.5 us -> 29.2 us (0.30)
  blocking collectives: 59.7 us -> 0 us
  Pallas kernels: 0 us -> 22.5 us
  matrix products: 11.7 us -> 0 us
  other arithmetic: 7.45 us -> 0 us
  loops' own time: 5.72 us -> 0 us
  local copies, waits for them, and re-layouts: 8.39 us -> 4.79 us
  between operations: 4.16 us -> 1.35 us
    all_gather x2 -> x0, blocking collectives: 36.6 us -> none  [the longest x1 31.3 us: per_device(): lax.all_gather(full_views, 'blk', axis=0, tiled=True)]
    unnamed x1 -> x0, blocking collectives: 23.1 us -> none
    pallas_call x0 -> x1, Pallas kernels: none -> 22.5 us  [per_device(): pl.pallas_call(functools.partial(kernel, n, groups, tiles), out_shape=(ou...]
    dot_general x24 -> x0, matrix products: 11.7 us -> none  [the longest x8 5.39 us: score_view(): jnp.einsum('txk,yk->txy', part_b, sin_y, preferred_element_type=jnp.float32)]
    another operation x1 -> x0, loops' own time: 5.72 us -> none  [per_device(): lax.scan(score_view, start_state, (lax.all_gather(full_views, 'blk', axis...]
    convert_element_type x19 -> x0, other arithmetic: 5.47 us -> none  [the longest x8 4.48 us: score_view(): (transfer * (real_part * micro_real + imag_part * micro_imag)).astype(jnp...]
    dynamic_slice x8 -> x0, local copies, waits for them, and re-layouts: 4.71 us -> none  [per_device(): lax.scan(score_view, start_state, (lax.all_gather(full_views, 'blk', axis...]
    div x9 -> x0, other arithmetic: 1.33 us -> none  [the longest x1 0.7 us: per_device(): zscore_map = (peak_map - mean_map) / jnp.sqrt(variance + 1e-05)]
where the time goes in v1:
time: 29.2 us; the launch traced here: 28.6 us
  Pallas kernels  22.5 us (77%)
  local copies, waits for them, and re-layouts  4.79 us (16%)
  between operations  1.35 us (5%)
    pallas_call x1, Pallas kernels, per_device(): pl.pallas_call(functools.partial(kernel, n, groups, tiles), out_shape=(ou...  22.5 us
    unnamed x14, local copies, waits for them, and re-layouts  4.79 us

profile of v1, /device:TPU:0, one launch (start us, length us, event | category | flops | bytes accessed | tf_op | source)
XLA Modules:
  0.0 28.6 jit_solution(7770127432883811635)
XLA Ops:
  0.6 0.0 copy-start.5
  0.6 0.0 copy-start.4
  1.3 0.0 copy-done.5
  1.3 0.0 copy-done.4
  1.3 0.0 copy-start
  1.3 0.9 %copy-done = bf16[4,128,256]{2,1,0:T(8,128)(2,1)S(1)} copy-done((bf16[4,128,256]{2,1,0:T(8,128)(2,1)S(1)}, bf16[4,128,256]{2,1,0:T(8,128)(2,1)}, u32[]{:S(2)}) %copy-start) | copy-done | bytes 262168
  2.3 0.0 copy-start.1
  2.3 0.9 %copy-done.1 = bf16[2,2,128,128]{3,2,1,0:T(8,128)(2,1)S(1)} copy-done((bf16[2,2,128,128]{3,2,1,0:T(8,128)(2,1)S(1)}, bf16[2,2,128,128]{3,2,1,0:T(8,128)(2,1)}, u32[]{:S(2)}) %copy-start.1) | copy-done | bytes 131096
  3.2 0.0 copy-start.2
  3.2 0.9 %copy-done.2 = bf16[256,256]{1,0:T(8,128)(2,1)S(1)} copy-done((bf16[256,256]{1,0:T(8,128)(2,1)S(1)}, bf16[256,256]{1,0:T(8,128)(2,1)}, u32[]{:S(2)}) %copy-start.2) | copy-done | bytes 131096
  4.1 0.0 copy-start.3
  4.1 0.7 %copy-done.3 = bf16[1,2,32,128]{3,2,1,0:T(8,128)(2,1)S(1)} copy-done((bf16[1,2,32,128]{3,2,1,0:T(8,128)(2,1)S(1)}, bf16[1,2,32,128]{3,2,1,0:T(8,128)(2,1)}, u32[]{:S(2)}) %copy-start.3) | copy-done | bytes 16408
  4.8 22.5 %shard_map.86 = (f32[2,64,256]{2,1,0:T(8,128)S(1)}, f32[2,64,256]{2,1,0:T(8,128)S(1)}) custom-call(bf16[1,2,32,128]{3,2,1,0:T(8,128)(2,1)S(1)} %copy-done.3, s32[1]{0:T(128)S(6)} %copy.11.states_ref, bf16[2,2,128,128]{3,2,1,0:T(8,128)(2,1)S(1)} %copy-done.1, f32[8]{0:T(128)S(1)} %copy-done.4, s32[2]{0:T(128)S(1)} %copy-done.5, ...), custom_call_target="tpu_custom_call" | custom-call | tf_op jit(solution)/shard_map/pallas_call | solution.py:260
  27.3 0.7 %copy.12 = f32[2,64,256]{2,1,0:T(8,128)} copy(f32[2,64,256]{2,1,0:T(8,128)S(1)} %get-tuple-element.4) | data formatting | bytes 262144
  27.9 0.7 %copy.13 = f32[2,64,256]{2,1,0:T(8,128)} copy(f32[2,64,256]{2,1,0:T(8,128)S(1)} %get-tuple-element.5) | data formatting | bytes 262144
Async XLA Ops:
  0.6 0.7 %copy-start.5 = (s32[2]{0:T(128)S(1)}, s32[2]{0:T(128)}, u32[]{:S(2)}) copy-start(s32[2]{0:T(128)} %group_ref.1) | copy-start | bytes 28
  0.6 0.7 %copy-start.4 = (f32[8]{0:T(128)S(1)}, f32[8]{0:T(128)}, u32[]{:S(2)}) copy-start(f32[8]{0:T(128)} %defocus_ref.1) | copy-start | bytes 100
  1.3 1.0 %copy-start = (bf16[4,128,256]{2,1,0:T(8,128)(2,1)S(1)}, bf16[4,128,256]{2,1,0:T(8,128)(2,1)}, u32[]{:S(2)}) copy-start(bf16[4,128,256]{2,1,0:T(8,128)(2,1)} %constant.4.clone.left_ref) | copy-start | bytes 786436
  2.3 0.9 %copy-start.1 = (bf16[2,2,128,128]{3,2,1,0:T(8,128)(2,1)S(1)}, bf16[2,2,128,128]{3,2,1,0:T(8,128)(2,1)}, u32[]{:S(2)}) copy-start(bf16[2,2,128,128]{3,2,1,0:T(8,128)(2,1)} %micro_ref.1) | copy-start | bytes 393220
  3.2 0.9 %copy-start.2 = (bf16[256,256]{1,0:T(8,128)(2,1)S(1)}, bf16[256,256]{1,0:T(8,128)(2,1)}, u32[]{:S(2)}) copy-start(bf16[256,256]{1,0:T(8,128)(2,1)} %constant.5.clone.right_ref) | copy-start | bytes 393220
  4.1 0.7 %copy-start.3 = (bf16[1,2,32,128]{3,2,1,0:T(8,128)(2,1)S(1)}, bf16[1,2,32,128]{3,2,1,0:T(8,128)(2,1)}, u32[]{:S(2)}) copy-start(bf16[1,2,32,128]{3,2,1,0:T(8,128)(2,1)} %views_ref.1) | copy-start | bytes 49156

commit v2 on v1

--- a/solution.py
+++ b/solution.py
@@ -37,15 +37,35 @@
     return np.stack(left).astype(ml_dtypes.bfloat16), right.astype(ml_dtypes.bfloat16)
 
 
-def flip_bits(index, mask, size):
-    bits = int(math.log2(size))
-    return sum(((index // 2**i + mask // 2**i) % 2) * 2**i for i in range(bits))
+def flip_bits(bits, mask):
+    return sum(lax.rem(bit + lax.rem(lax.div(mask, 2**i), 2), 2) * 2**i for i, bit in enumerate(bits))
+
+
+def sine(x):
+    turns = jnp.round(x * (1.0 / math.pi))
+    r = (x - turns * 3.140625) - turns * (math.pi - 3.140625)
+    half = turns * 0.5
+    sign = 1.0 - 4.0 * jnp.abs(half - jnp.floor(half))
+    r2 = r * r
+    poly = -2.5052108e-8
+    for c in (2.7557319e-6, -1.9841270e-4, 8.3333333e-3, -1.6666667e-1):
+        poly = poly * r2 + c
+    return sign * (r + r * (r2 * poly))
 
 
 def kernel(
     n,
     groups,
     tiles,
+    views_hbm,
+    states_hbm,
+    micro_hbm,
+    defocus_hbm,
+    group_hbm,
+    left_hbm,
+    right_hbm,
+    peak_ref,
+    zscore_ref,
     views_ref,
     states_ref,
     micro_ref,
@@ -53,8 +73,7 @@
     group_ref,
     left_ref,
     right_ref,
-    peak_ref,
-    zscore_ref,
+    fetch_sem,
     spectra,
     flags,
     filtered,
@@ -64,12 +83,8 @@
     blk_recv,
     flag_send,
     flag_recv,
-    x_send,
-    x_recv,
     core_send,
     core_recv,
-    far_send,
-    far_recv,
 ):
     b, g = lax.axis_index("blk"), lax.axis_index("grp")
     g_core = g + 1 - 2 * (g % 2)
@@ -86,16 +101,24 @@
         else:
             lax.fori_loop(low, high, lambda d, carry: (body(d), carry)[1], 0)
 
+    bits = [lax.rem(lax.div(b, 2**i), 2) for i in range(int(math.log2(n)))]
+    peers = []
+    if unroll:
+        for d in range(n):
+            signs = [(1 - 2 * bit) * 2**i for i, bit in enumerate(bits) if d >> i & 1]
+            peers.append(sum(signs, b))
+
     def peer(d):
-        return flip_bits(b, d, n)
+        return peers[d] if unroll else flip_bits(bits, d)
 
     def to(block, group):
         return dict(device_id=(block, group), device_id_type=MESH)
 
-    def blk_copy(d, source):
-        part = spectra.at[source, g]
+    def direct_copy(d, side, block, group):
+        part = spectra.at[block, group]
+        i = 2 * d + side
         return pltpu.make_async_remote_copy(
-            part, part, blk_send.at[d], blk_recv.at[d], **to(peer(d), g)
+            part, part, blk_send.at[i], blk_recv.at[i], **to(peer(d), g_x if side else g)
         )
 
     def flag_copy(d, source):
@@ -104,69 +127,80 @@
             part, part, flag_send.at[d], flag_recv.at[d], **to(peer(d), g)
         )
 
-    def x_copy(d, group):
+    def core_copy(d, side, group):
         part = spectra.at[peer(d), group]
+        i = 2 * d + side
         return pltpu.make_async_remote_copy(
-            part, part, x_send.at[d], x_recv.at[d], **to(b, g_x)
-        )
-
-    def core_copy(d, group):
-        part = spectra.at[peer(d), group]
-        return pltpu.make_async_remote_copy(
-            part, part, core_send.at[d], core_recv.at[d], **to(b, g_core)
-        )
-
-    def far_copy(d, group):
-        part = spectra.at[peer(d), group]
-        return pltpu.make_async_remote_copy(
-            part, part, far_send.at[d], far_recv.at[d], **to(b, g_core)
-        )
-
+            part, part, core_send.at[i], core_recv.at[i], **to(b, g_core)
+        )
+
+    fetches = [
+        pltpu.make_async_copy(source, target, fetch_sem.at[i])
+        for i, (source, target) in enumerate(
+            [
+                (states_hbm, states_ref),
+                (views_hbm, views_ref),
+                (group_hbm, group_ref),
+                (defocus_hbm, defocus_ref),
+                (micro_hbm, micro_ref),
+                (left_hbm.at[g], left_ref),
+                (right_hbm, right_ref),
+            ]
+        )
+    ]
     barrier = pltpu.get_barrier_semaphore()
     each(1, n, lambda d: pl.semaphore_signal(barrier, inc=1, **to(peer(d), g)))
-    pl.semaphore_signal(barrier, inc=1, **to(b, g_x))
+    each(0, n, lambda d: pl.semaphore_signal(barrier, inc=1, **to(peer(d), g_x)))
     pl.semaphore_signal(barrier, inc=1, **to(b, g_core))
+    for fetch in fetches:
+        fetch.start()
+    for fetch in fetches[:2]:
+        fetch.wait()
 
     state = states_ref[0]
     flip = (1 - 2 * (state % 2)).astype(f32)
     spectra[b, g, 0] = views_ref[0, 0]
     spectra[b, g, 1] = (views_ref[0, 1].astype(f32) * flip).astype(bf16)
     flags[b] = jnp.full((1, KF), (state // 2).astype(f32), f32)
-    pl.semaphore_wait(barrier, n + 1)
-
-    x_copy(0, g).start()
-    core_copy(0, g).start()
-
-    def send_own(d):
-        blk_copy(d, b).start()
+    pl.semaphore_wait(barrier, 2 * n)
+
+    def send_own(i):
+        d = n - 1 - i
+        direct_copy(d, 0, b, g).start()
+        direct_copy(d, 1, b, g).start()
         flag_copy(d, b).start()
 
-    each(1, n, send_own)
-
+    core_copy(0, 0, g).start()
+    each(0, n - 1, send_own)
+    direct_copy(0, 1, b, g).start()
+
+    for fetch in fetches[2:]:
+        fetch.wait()
     micro = (b * tiles) // (n * tiles // MICROGRAPHS)
     base = defocus_ref[group_ref[micro]]
     row_f = (lax.broadcasted_iota(jnp.int32, (KF, KF), 0) - KF // 2).astype(f32)
     col_f = (lax.broadcasted_iota(jnp.int32, (KF, KF), 1) - KF // 2).astype(f32)
     radius_sq = (row_f * row_f + col_f * col_f) * (1.0 / (KF * KF))
     for step in range(2):
-        transfer = -jnp.sin((base + focus_offset * (2.0 * step - 1.0)) * radius_sq + phase_shift)
+        transfer = -sine((base + focus_offset * (2.0 * step - 1.0)) * radius_sq + phase_shift)
         for t in range(tiles):
             for part in range(2):
                 filtered[step, t, part] = transfer * micro_ref[t, part].astype(f32)
 
-    def forward_blk(d):
-        blk_copy(d, peer(d)).wait_recv()
-        x_copy(d, g).start()
-        core_copy(d, g).start()
-
-    def forward_x(d):
-        x_copy(d, g_x).wait_recv()
-        far_copy(d, g_x).start()
+    def forward(d, side):
+        group = g_x if side else g
+        direct_copy(d, side, peer(d), group).wait_recv()
+        core_copy(d, side, group).start()
+
+    def forward_both(d):
+        forward(d, 0)
+        forward(d, 1)
+        wait_flag(d)
 
     def score(d, first):
         v = peer(d)
-        core_copy(d, g_core).wait_recv()
-        far_copy(d, g_far).wait_recv()
+        core_copy(d, 0, g_core).wait_recv()
+        core_copy(d, 1, g_far).wait_recv()
         real = spectra[v, :, 0].reshape(KF, KF).astype(f32)
         imag = spectra[v, :, 1].reshape(KF, KF).astype(f32)
         later = jnp.broadcast_to(flags[v], (KF, KF)) > 0.5
@@ -178,7 +212,7 @@
             prod_imag = (real * m_imag - imag * m_real).astype(bf16)
             stacks.append(jnp.concatenate([prod_real, prod_imag], axis=0))
         stacked = jnp.concatenate(stacks, axis=1)
-        section = jnp.dot(left_ref[g], stacked, preferred_element_type=f32).astype(bf16)
+        section = jnp.dot(left_ref[...], stacked, preferred_element_type=f32).astype(bf16)
         lines = jnp.concatenate(
             [
                 jnp.concatenate(
@@ -206,27 +240,10 @@
     def wait_flag(d):
         flag_copy(d, peer(d)).wait_recv()
 
-    if unroll:
-        for d in range(n + 2):
-            if 1 <= d < n:
-                forward_blk(d)
-            if 1 <= d <= n:
-                forward_x(d - 1)
-            if d >= 2:
-                if d > 2:
-                    wait_flag(d - 2)
-                score(d - 2, d == 2)
-    else:
-        forward_x(0)
-
-        def pump(d):
-            forward_blk(d)
-            wait_flag(d)
-
-        each(1, n, pump)
-        each(1, n, forward_x)
-        score(0, True)
-        each(1, n, lambda d: score(d, False))
+    forward(0, 1)
+    each(1, n, forward_both)
+    score(0, True)
+    each(1, n, lambda d: score(d, False))
 
     total = 1.0 / n
     mean = totals[...] * total
@@ -234,12 +251,12 @@
     zscore_ref[...] = (peak_ref[...] - mean) * lax.rsqrt(variance + 1e-5)
 
     def drain(d):
-        x_copy(d, g).wait_send()
-        core_copy(d, g).wait_send()
-        far_copy(d, g_x).wait_send()
+        core_copy(d, 0, g).wait_send()
+        core_copy(d, 1, g_x).wait_send()
+        direct_copy(d, 1, b, g).wait_send()
 
     def drain_own(d):
-        blk_copy(d, b).wait_send()
+        direct_copy(d, 0, b, g).wait_send()
         flag_copy(d, b).wait_send()
 
     each(0, n, drain)
@@ -255,23 +272,31 @@
         rows = view_spectra.shape[2]
         columns = BOX // groups
         vmem = pl.BlockSpec(memory_space=pltpu.VMEM)
-        smem = pl.BlockSpec(memory_space=pltpu.SMEM)
+        hbm = pl.BlockSpec(memory_space=pltpu.HBM)
         out = jax.ShapeDtypeStruct((tiles, columns, BOX), f32)
         return pl.pallas_call(
             functools.partial(kernel, n, groups, tiles),
             out_shape=(out, out),
-            in_specs=[vmem, smem, vmem, smem, smem, vmem, vmem],
+            in_specs=[hbm] * 7,
             out_specs=(vmem, vmem),
             scratch_shapes=[
+                pltpu.VMEM(view_spectra.shape, bf16),
+                pltpu.SMEM(search_states.shape, jnp.int32),
+                pltpu.VMEM(micrograph_spectra.shape, bf16),
+                pltpu.SMEM(defocus.shape, f32),
+                pltpu.SMEM(micrograph_group.shape, jnp.int32),
+                pltpu.VMEM(left.shape[1:], bf16),
+                pltpu.VMEM(right.shape, bf16),
+                pltpu.SemaphoreType.DMA((7,)),
                 pltpu.VMEM((n, groups, 2, rows, KF), bf16),
                 pltpu.VMEM((n, 1, KF), f32),
                 pltpu.VMEM((2, tiles, 2, KF, KF), f32),
                 pltpu.VMEM((tiles, columns, BOX), f32),
                 pltpu.VMEM((tiles, columns, BOX), f32),
             ]
-            + [pltpu.SemaphoreType.DMA((n,))] * 10,
+            + [pltpu.SemaphoreType.DMA((2 * n,))] * 6,
             compiler_params=pltpu.CompilerParams(
-                collective_id=0, has_side_effects=True, vmem_limit_bytes=32 * 2**20
+                collective_id=0, has_side_effects=True, vmem_limit_bytes=60 * 2**20
             ),
         )(
             view_spectra,

time: 29.2 us -> 21.9 us (0.75); the launches traced: 28.6 us -> 21.6 us
  Pallas kernels: 22.5 us -> 18.1 us
  local copies, waits for them, and re-layouts: 4.79 us -> 2.26 us
    pallas_call x1, Pallas kernels: 22.5 us -> 18.1 us  [per_device(): pl.pallas_call(functools.partial(kernel, n, groups, tiles), out_shape=(ou...]
    unnamed x14 -> x4, local copies, waits for them, and re-layouts: 4.79 us -> 2.26 us
where the time goes in v2:
time: 21.9 us; the launch traced here: 21.6 us
  Pallas kernels  18.1 us (83%)
  local copies, waits for them, and re-layouts  2.26 us (10%)
  between operations  1.29 us (6%)
    pallas_call x1, Pallas kernels, per_device(): pl.pallas_call(functools.partial(kernel, n, groups, tiles), out_shape=(ou...  18.1 us
    unnamed x4, local copies, waits for them, and re-layouts  2.26 us

profile of v2, /device:TPU:0, one launch (start us, length us, event | category | flops | bytes accessed | tf_op | source)
XLA Modules:
  0.0 21.6 jit_solution(11282381922641629095)
XLA Ops:
  1.3 18.1 %shard_map.86 = (f32[2,64,256]{2,1,0:T(8,128)}, f32[2,64,256]{2,1,0:T(8,128)}) custom-call(bf16[1,2,32,128]{3,2,1,0:T(8,128)(2,1)} %views_hbm.1, s32[1]{0:T(128)S(6)} %copy.11.states_hbm, bf16[2,2,128,128]{3,2,1,0:T(8,128)(2,1)} %micro_hbm.1, f32[8]{0:T(128)} %defocus_hbm.1, s32[2]{0:T(128)} %group_hbm.1, bf16[4,128,256]{2,1,0:T(8,128)(2,1)} %constant.4.clone.left_hbm, ...), custom_call_target="tpu_custom_call" | custom-call | tf_op jit(solution)/shard_map/pallas_call | solution.py:277
  19.4 0.0 copy-start
  19.4 1.6 %copy.12 = f32[2,64,256]{2,1,0:T(8,128)} copy(f32[2,64,256]{2,1,0:T(8,128)} %get-tuple-element.4) | data formatting | bytes 262144
  21.0 0.0 copy-done
  21.0 0.7 %copy.13 = f32[2,64,256]{2,1,0:T(8,128)} copy(f32[2,64,256]{2,1,0:T(8,128)S(1)} %copy-done) | data formatting | bytes 262144
Async XLA Ops:
  19.4 1.6 %copy-start = (f32[2,64,256]{2,1,0:T(8,128)S(1)}, f32[2,64,256]{2,1,0:T(8,128)}, u32[]{:S(2)}) copy-start(f32[2,64,256]{2,1,0:T(8,128)} %get-tuple-element.5) | copy-start | bytes 393220

commit v3 on v2

--- a/solution.py
+++ b/solution.py
@@ -57,17 +57,17 @@
     n,
     groups,
     tiles,
+    states_ref,
     views_hbm,
-    states_hbm,
     micro_hbm,
     defocus_hbm,
     group_hbm,
     left_hbm,
     right_hbm,
     peak_ref,
-    zscore_ref,
+    totals,
+    squares,
     views_ref,
-    states_ref,
     micro_ref,
     defocus_ref,
     group_ref,
@@ -77,8 +77,6 @@
     spectra,
     flags,
     filtered,
-    totals,
-    squares,
     blk_send,
     blk_recv,
     flag_send,
@@ -138,7 +136,6 @@
         pltpu.make_async_copy(source, target, fetch_sem.at[i])
         for i, (source, target) in enumerate(
             [
-                (states_hbm, states_ref),
                 (views_hbm, views_ref),
                 (group_hbm, group_ref),
                 (defocus_hbm, defocus_ref),
@@ -154,7 +151,7 @@
     pl.semaphore_signal(barrier, inc=1, **to(b, g_core))
     for fetch in fetches:
         fetch.start()
-    for fetch in fetches[:2]:
+    for fetch in fetches[:1]:
         fetch.wait()
 
     state = states_ref[0]
@@ -174,7 +171,7 @@
     each(0, n - 1, send_own)
     direct_copy(0, 1, b, g).start()
 
-    for fetch in fetches[2:]:
+    for fetch in fetches[1:]:
         fetch.wait()
     micro = (b * tiles) // (n * tiles // MICROGRAPHS)
     base = defocus_ref[group_ref[micro]]
@@ -245,11 +242,6 @@
     score(0, True)
     each(1, n, lambda d: score(d, False))
 
-    total = 1.0 / n
-    mean = totals[...] * total
-    variance = squares[...] * total - mean * mean
-    zscore_ref[...] = (peak_ref[...] - mean) * lax.rsqrt(variance + 1e-5)
-
     def drain(d):
         core_copy(d, 0, g).wait_send()
         core_copy(d, 1, g_x).wait_send()
@@ -261,6 +253,13 @@
 
     each(0, n, drain)
     each(1, n, drain_own)
+
+
+def finish(n, best_ref, totals_ref, squares_ref, peak_ref, zscore_ref):
+    mean = totals_ref[...] * (1.0 / n)
+    variance = squares_ref[...] * (1.0 / n) - mean * mean
+    peak_ref[...] = best_ref[...]
+    zscore_ref[...] = (best_ref[...] - mean) * lax.rsqrt(variance + 1e-5)
 
 
 def solution(mesh):
@@ -274,39 +273,47 @@
         vmem = pl.BlockSpec(memory_space=pltpu.VMEM)
         hbm = pl.BlockSpec(memory_space=pltpu.HBM)
         out = jax.ShapeDtypeStruct((tiles, columns, BOX), f32)
-        return pl.pallas_call(
+        sums = pl.pallas_call(
             functools.partial(kernel, n, groups, tiles),
-            out_shape=(out, out),
-            in_specs=[hbm] * 7,
-            out_specs=(vmem, vmem),
+            out_shape=(pltpu.VMEM(out.shape, f32),) * 3,
+            in_specs=[pl.BlockSpec(memory_space=pltpu.SMEM)] + [hbm] * 6,
+            out_specs=(vmem,) * 3,
             scratch_shapes=[
                 pltpu.VMEM(view_spectra.shape, bf16),
-                pltpu.SMEM(search_states.shape, jnp.int32),
                 pltpu.VMEM(micrograph_spectra.shape, bf16),
                 pltpu.SMEM(defocus.shape, f32),
                 pltpu.SMEM(micrograph_group.shape, jnp.int32),
                 pltpu.VMEM(left.shape[1:], bf16),
                 pltpu.VMEM(right.shape, bf16),
-                pltpu.SemaphoreType.DMA((7,)),
+                pltpu.SemaphoreType.DMA((6,)),
                 pltpu.VMEM((n, groups, 2, rows, KF), bf16),
                 pltpu.VMEM((n, 1, KF), f32),
                 pltpu.VMEM((2, tiles, 2, KF, KF), f32),
-                pltpu.VMEM((tiles, columns, BOX), f32),
-                pltpu.VMEM((tiles, columns, BOX), f32),
             ]
             + [pltpu.SemaphoreType.DMA((2 * n,))] * 6,
             compiler_params=pltpu.CompilerParams(
-                collective_id=0, has_side_effects=True, vmem_limit_bytes=60 * 2**20
+                collective_id=0, has_side_effects=True, vmem_limit_bytes=24 * 2**20
             ),
         )(
-            view_spectra,
             search_states,
-            micrograph_spectra,
-            defocus,
-            micrograph_group,
-            jnp.asarray(left),
-            jnp.asarray(right),
-        )
+            *(
+                pltpu.with_memory_space_constraint(x, pltpu.HBM)
+                for x in (
+                    view_spectra,
+                    micrograph_spectra,
+                    defocus,
+                    micrograph_group,
+                    jnp.asarray(left),
+                    jnp.asarray(right),
+                )
+            )
+        )
+        return pl.pallas_call(
+            functools.partial(finish, n),
+            out_shape=(out, out),
+            in_specs=[vmem] * 3,
+            out_specs=(vmem, vmem),
+        )(*(pltpu.with_memory_space_constraint(x, pltpu.VMEM) for x in sums))
 
     return jax.shard_map(
         per_device,

time: 21.9 us -> 19.6 us (0.89)
  local copies, waits for them, and re-layouts: 2.26 us -> 0 us
    unnamed x4 -> x0, local copies, waits for them, and re-layouts: 2.26 us -> none
    pallas_call x1 -> x2, Pallas kernels: 18.1 us -> 18.1 us  [the longest x1 17.4 us: per_device(): pl.pallas_call(functools.partial(kernel, n, groups, tiles), out_shape=(pl...]
where the time goes in v3:
time: 19.6 us; the launch traced here: 19.4 us
  Pallas kernels  18.1 us (92%)
  between operations  1.28 us (7%)
    pallas_call x1, Pallas kernels, per_device(): pl.pallas_call(functools.partial(kernel, n, groups, tiles), out_shape=(pl...  17.4 us
    pallas_call x1, Pallas kernels, per_device(): pl.pallas_call(functools.partial(finish, n), out_shape=(out, out), in_spe...  0.71 us

profile of v3, /device:TPU:0, one launch (start us, length us, event | category | flops | bytes accessed | tf_op | source)
XLA Modules:
  0.0 19.4 jit_solution(414957002414629923)
XLA Ops:
  1.3 17.4 %shard_map.86 = (f32[2,64,256]{2,1,0:T(8,128)S(1)}, f32[2,64,256]{2,1,0:T(8,128)S(1)}, f32[2,64,256]{2,1,0:T(8,128)S(1)}) custom-call(s32[1]{0:T(128)S(6)} %copy.9.states_ref, bf16[1,2,32,128]{3,2,1,0:T(8,128)(2,1)} %views_hbm.1, bf16[2,2,128,128]{3,2,1,0:T(8,128)(2,1)} %micro_hbm.1, f32[8]{0:T(128)} %defocus_hbm.1, s32[2]{0:T(128)} %group_hbm.1, ...), custom_call_target="tpu_custom_call" | custom-call | tf_op jit(solution)/shard_map/pallas_call | solution.py:276
  18.6 0.7 %shard_map.87 = (f32[2,64,256]{2,1,0:T(8,128)}, f32[2,64,256]{2,1,0:T(8,128)}) custom-call(f32[2,64,256]{2,1,0:T(8,128)S(1)} %get-tuple-element.5.best_ref, f32[2,64,256]{2,1,0:T(8,128)S(1)} %get-tuple-element.6.totals_ref, f32[2,64,256]{2,1,0:T(8,128)S(1)} %get-tuple-element.7.squares_ref), custom_call_target="tpu_custom_call" | custom-call | tf_op jit(solution)/shard_map/pallas_call | solution.py:311

commit v4 on v3

--- a/solution.py
+++ b/solution.py
@@ -162,14 +162,14 @@
     pl.semaphore_wait(barrier, 2 * n)
 
     def send_own(i):
-        d = n - 1 - i
+        d = i + 1
         direct_copy(d, 0, b, g).start()
         direct_copy(d, 1, b, g).start()
         flag_copy(d, b).start()
 
+    direct_copy(0, 1, b, g).start()
     core_copy(0, 0, g).start()
     each(0, n - 1, send_own)
-    direct_copy(0, 1, b, g).start()
 
     for fetch in fetches[1:]:
         fetch.wait()
@@ -238,9 +238,16 @@
         flag_copy(d, peer(d)).wait_recv()
 
     forward(0, 1)
-    each(1, n, forward_both)
-    score(0, True)
-    each(1, n, lambda d: score(d, False))
+    if unroll:
+        for d in range(1, n + 2):
+            if d < n:
+                forward_both(d)
+            if d >= 2:
+                score(d - 2, d == 2)
+    else:
+        each(1, n, forward_both)
+        score(0, True)
+        each(1, n, lambda d: score(d, False))
 
     def drain(d):
         core_copy(d, 0, g).wait_send()

time: 19.6 us -> 18.1 us (0.923)
  Pallas kernels: 18.1 us -> 16.6 us
    pallas_call x1, Pallas kernels: 17.4 us -> 15.8 us  [per_device(): pl.pallas_call(functools.partial(kernel, n, groups, tiles), out_shape=(pl...]
where the time goes in v4:
time: 18.1 us; the launch traced here: 17.8 us
  Pallas kernels  16.6 us (92%)
  between operations  1.28 us (7%)
    pallas_call x1, Pallas kernels, per_device(): pl.pallas_call(functools.partial(kernel, n, groups, tiles), out_shape=(pl...  15.8 us
    pallas_call x1, Pallas kernels, per_device(): pl.pallas_call(functools.partial(finish, n), out_shape=(out, out), in_spe...  0.71 us

profile of v4, /device:TPU:0, one launch (start us, length us, event | category | flops | bytes accessed | tf_op | source)
XLA Modules:
  0.0 17.8 jit_solution(17317762648191827581)
XLA Ops:
  1.3 15.8 %shard_map.86 = (f32[2,64,256]{2,1,0:T(8,128)S(1)}, f32[2,64,256]{2,1,0:T(8,128)S(1)}, f32[2,64,256]{2,1,0:T(8,128)S(1)}) custom-call(s32[1]{0:T(128)S(6)} %copy.9.states_ref, bf16[1,2,32,128]{3,2,1,0:T(8,128)(2,1)} %views_hbm.1, bf16[2,2,128,128]{3,2,1,0:T(8,128)(2,1)} %micro_hbm.1, f32[8]{0:T(128)} %defocus_hbm.1, s32[2]{0:T(128)} %group_hbm.1, ...), custom_call_target="tpu_custom_call" | custom-call | tf_op jit(solution)/shard_map/pallas_call | solution.py:283
  17.1 0.7 %shard_map.87 = (f32[2,64,256]{2,1,0:T(8,128)}, f32[2,64,256]{2,1,0:T(8,128)}) custom-call(f32[2,64,256]{2,1,0:T(8,128)S(1)} %get-tuple-element.5.best_ref, f32[2,64,256]{2,1,0:T(8,128)S(1)} %get-tuple-element.6.totals_ref, f32[2,64,256]{2,1,0:T(8,128)S(1)} %get-tuple-element.7.squares_ref), custom_call_target="tpu_custom_call" | custom-call | tf_op jit(solution)/shard_map/pallas_call | solution.py:318
